TPU v7x, 32 devices: a whole 2x2x4 slice. The times are simulated.
32 devices in a mesh: parts: 2 (over y), row: 4 (over z), col: 4 (over x, core).
Axes of the slice: x: 2, y: 2, z: 4, core: 2. Of those that a mesh axis runs over, the one named last changes fastest.
Arguments:
- pair: float32 [192, 96, 128], P(('parts', 'row'), 'col'), parts along dimension 0, may hold values from -6 to 6
- chain: int32 [192], P('parts'), parts along dimension 0, may hold values from 0 to 3, never falling along the last dimension, each value on 1 to 48 neighbouring positions
- block_mask: int32 [24, 12], P('parts'), parts along dimension 0, may hold values 0 or 1
- norm_gain: float32 [5, 128], replicated, may hold values from 0.1 to 1.9
- norm_bias: float32 [5, 128], replicated, may hold values from -3 to 3
- w_proj: bfloat16 [2, 128, 640], replicated, may hold values from -0.5 to 0.5
- w_out: bfloat16 [2, 128, 128], replicated, may hold values from -0.5 to 0.5
- w_trans_in: bfloat16 [128, 1024], replicated, may hold values from -0.5 to 0.5
- w_trans_out: bfloat16 [512, 128], replicated, may hold values from -0.25 to 0.25
Outputs:
- pair_out: float32 [192, 96, 128], P(('parts', 'row'), 'col'), parts along dimension 0
There are 2 independent parts, one for each index of `parts`. A program takes and returns all parts, laid end to end along the dimension named above; an argument that names none is the same for every part. Nothing has to cross between parts.
Inputs may be any that keep to these rules, and one draw needn't show every extreme that they name: Chain ids never fall along the residues; one chain has exactly 48 residues and none has more.
All inputs are finite; a program needn't handle non-finite values.
Results may differ from a plain program's by a relative error of at most 0.0057.
Values may be sent and summed in bfloat16 or wider, within the bound.
A program may use at most 64 MiB of HBM per device.

v0:
```python
import jax
import jax.numpy as jnp
from jax import lax
from jax.sharding import PartitionSpec as P

MASK_TILE = 8


def broadcast(array, axis, root):
    mine = lax.axis_index(axis) == root
    return lax.psum(jnp.where(mine, array, jnp.zeros_like(array)), axis)


def layer_norm(values, gain, bias):
    center = jnp.mean(values, axis=-1, keepdims=True)
    spread = jnp.mean((values - center) ** 2, axis=-1, keepdims=True)
    return (values - center) * lax.rsqrt(spread + 1e-05) * gain + bias


def project_edges(state, pair_mask, norm_gain, norm_bias, w_proj, update):
    channels = state.shape[2]
    normed = layer_norm(state, norm_gain[2 * update], norm_bias[2 * update]).astype(jnp.bfloat16)
    proj = jnp.dot(normed, w_proj[update], preferred_element_type=jnp.float32)
    left_edge = (
        jax.nn.sigmoid(proj[..., 0:channels]) * proj[..., channels : 2 * channels] * pair_mask
    ).astype(jnp.bfloat16)
    right_edge = (
        jax.nn.sigmoid(proj[..., 2 * channels : 3 * channels])
        * proj[..., 3 * channels : 4 * channels]
        * pair_mask
    ).astype(jnp.bfloat16)
    gating = jax.nn.sigmoid(proj[..., 4 * channels :])
    return (left_edge, right_edge, gating)


def finish_update(state, triangle, gating, norm_gain, norm_bias, w_out, update):
    tri_norm = layer_norm(triangle, norm_gain[2 * update + 1], norm_bias[2 * update + 1]).astype(
        jnp.bfloat16
    )
    return state + gating * jnp.dot(tri_norm, w_out[update], preferred_element_type=jnp.float32)


def local(pair, chain, block_mask, norm_gain, norm_bias, w_proj, w_out, w_trans_in, w_trans_out):
    extent = pair.shape[0]
    row_offset = lax.axis_index("row") * extent
    col_offset = lax.axis_index("col") * extent
    row_chain = lax.dynamic_slice_in_dim(chain, row_offset, extent)
    col_chain = lax.dynamic_slice_in_dim(chain, col_offset, extent)
    expanded = jnp.repeat(jnp.repeat(block_mask, MASK_TILE, axis=0), MASK_TILE, axis=1)
    local_blocks = lax.dynamic_slice(expanded, (row_offset, col_offset), (extent, extent)) > 0
    same_chain = row_chain[:, None] == col_chain[None, :]
    pair_mask = jnp.logical_or(same_chain, local_blocks).astype(jnp.float32)[..., None]
    state = pair
    left_edge, right_edge, gating = project_edges(state, pair_mask, norm_gain, norm_bias, w_proj, 0)
    right_strip = lax.all_gather(right_edge, "col", axis=1, tiled=True)
    mirrored_right = broadcast(right_strip, "row", lax.axis_index("col"))
    partner = mirrored_right
    triangle = jnp.einsum(
        "ikc,jkc->ijc",
        lax.all_gather(left_edge, "col", axis=1, tiled=True),
        partner,
        preferred_element_type=jnp.float32,
    )
    state = finish_update(state, triangle, gating, norm_gain, norm_bias, w_out, 0)
    left_edge, right_edge, gating = project_edges(state, pair_mask, norm_gain, norm_bias, w_proj, 1)
    left_strip = lax.all_gather(left_edge, "row", axis=0, tiled=True)
    mirrored_left = broadcast(left_strip, "col", lax.axis_index("row"))
    partner = mirrored_left
    triangle = jnp.einsum(
        "kic,kjc->ijc",
        partner,
        lax.all_gather(right_edge, "row", axis=0, tiled=True),
        preferred_element_type=jnp.float32,
    )
    state = finish_update(state, triangle, gating, norm_gain, norm_bias, w_out, 1)
    trans_norm = layer_norm(state, norm_gain[4], norm_bias[4]).astype(jnp.bfloat16)
    hidden_pre = jnp.dot(trans_norm, w_trans_in, preferred_element_type=jnp.float32)
    width = w_trans_out.shape[0]
    activated = (jax.nn.silu(hidden_pre[..., :width]) * hidden_pre[..., width:]).astype(
        jnp.bfloat16
    )
    return state + jnp.dot(activated, w_trans_out, preferred_element_type=jnp.float32)


def solution(mesh):
    return jax.shard_map(
        local,
        mesh=mesh,
        in_specs=(
            P(("parts", "row"), "col", None),
            P("parts"),
            P("parts", None),
            P(),
            P(),
            P(),
            P(),
            P(),
            P(),
        ),
        out_specs=P(("parts", "row"), "col", None),
        check_vma=False,
    )
```

profile of v0, /device:TPU:0, one launch (start us, length us, event | category | flops | bytes accessed | tf_op | source)
XLA Modules:
  0.0 140.4 jit_solution(15287354675224022705)
XLA Ops:
  6.5 1.1 reduce_sum.90
  7.7 1.2 multiply_reduce_fusion.4
  10.7 0.9 slice_bitcast_fusion
  11.6 1.5 %fusion.34 = f32[24,24,640]{2,1,0:T(8,128)S(1)} fusion(bf16[2,128,640]{2,1,0:T(8,128)(2,1)} %param.14, f32[24,24,128]{2,1,0:T(8,128)} %param.9, f32[128]{0:T(128)S(1)} %get-tuple-element.17, f32[128]{0:T(128)S(1)} %get-tuple-element.30, f32[24,24]{1,0:T(8,128)S(1)} %add_rsqrt_fusion.4, f32[24,24]{1,0:T(8,128)S(1)} %broadcast_multiply_fusion.4), kind=kOutput, calls=%fused_computation.63 | convolution fusion | flops 94740480 | bytes 1938944 | tf_op jit(solution)/shard_map/dot_general | solution.py:23
  13.4 9.0 %all_gather.12 = bf16[24,96,128]{2,1,0:T(8,128)(2,1)S(1)} all-gather(bf16[24,24,128]{2,1,0:T(8,128)(2,1)S(1)} %get-tuple-element.8), channel_id=1, replica_groups=mesh['parts'=2,'row'=4,'col'=4] {'col'}, dimensions={1}, use_global_device_ids=true | all-gather | bytes 737280 | tf_op jit(solution)/shard_map/all_gather | solution.py:55
  22.3 0.9 broadcast_select_fusion.1
  23.3 7.6 %all_gather.13 = bf16[24,96,128]{2,1,0:T(8,128)(2,1)S(1)} all-gather(bf16[24,24,128]{2,1,0:T(8,128)(2,1)S(1)} %get-tuple-element.7), channel_id=1, replica_groups=mesh['parts'=2,'row'=4,'col'=4] {'col'}, dimensions={1}, use_global_device_ids=true | all-gather | bytes 737280 | tf_op jit(solution)/shard_map/all_gather | solution.py:60
  30.9 1.3 copy.77
  32.2 31.3 %all-reduce.3.cloned.1.call-done = bf16[24,96,128]{2,1,0:T(8,128)(2,1)} async-done(((bf16[24,96,128]{2,1,0:T(8,128)(2,1)}), bf16[24,96,128]{2,1,0:T(8,128)(2,1)}) %all-reduce.3.cloned.1.call-update) | async-done | bytes 589840 | tf_op jit(solution)/shard_map/psum | solution.py:11
  63.5 2.3 %copy.76 = bf16[24,96,128]{1,0,2:T(8,128)(2,1)} copy(bf16[24,96,128]{2,1,0:T(8,128)(2,1)} %all-reduce.3.cloned.1.call-done) | data formatting | bytes 1179648 | tf_op jit(solution)/shard_map/psum | solution.py:11
  65.9 1.9 %bitcast_reduce_fusion.1 = (f32[24,24]{0,1:T(8,128)S(1)}, f32[128,24,24]{2,1,0:T(8,128)S(1)}) fusion(bf16[24,96,128]{1,0,2:T(8,128)(2,1)} %copy.76, bf16[24,96,128]{1,0,2:T(8,128)(2,1)} %copy.77), kind=kOutput, calls=%fused_computation.1 | convolution fusion | flops 14228928 | bytes 1476864 | tf_op jit(solution)/shard_map/ikc,jkc->ijc/dot_general | solution.py:58
  67.9 1.2 copy.78
  69.1 1.3 multiply_reduce_fusion.3
  70.4 1.5 %fusion.67 = (f32[24,24]{1,0:T(8,128)S(1)}, f32[24,24,128]{2,1,0:T(8,128)S(1)}) fusion(f32[24,24,128]{2,1,0:T(8,128)} %param.9, bf16[2,128,128]{2,1,0:T(8,128)(2,1)S(1)} %copy-done.4, f32[128,24,24]{0,1,2:T(8,128)} %copy.78, f32[128]{0:T(128)S(1)} %get-tuple-element.16, f32[128]{0:T(128)S(1)} %get-tuple-element.31, f32[24,24]{1,0:T(8,128)S(1)} %add_rsqrt_fusion.3, ...), kind=kOutput, calls=%fused_computation.119 | convolution fusion | flops 19684800 | bytes 1240320 | tf_op jit(solution)/shard_map/dot_general | solution.py:40
  73.3 16.3 %all_gather.15 = bf16[96,24,128]{2,1,0:T(8,128)(2,1)S(1)} all-gather(bf16[24,24,128]{2,1,0:T(8,128)(2,1)S(1)} %get-tuple-element.5), channel_id=1, replica_groups=mesh['parts'=2,'row'=4,'col'=4] {'row'}, dimensions={0}, use_global_device_ids=true | all-gather | bytes 737280 | tf_op jit(solution)/shard_map/all_gather | solution.py:66
  90.2 0.9 broadcast_select_fusion
  91.2 15.0 %all_gather.14 = bf16[96,24,128]{2,1,0:T(8,128)(2,1)S(1)} all-gather(bf16[24,24,128]{2,1,0:T(8,128)(2,1)S(1)} %get-tuple-element.6), channel_id=1, replica_groups=mesh['parts'=2,'row'=4,'col'=4] {'row'}, dimensions={0}, use_global_device_ids=true | all-gather | bytes 737280 | tf_op jit(solution)/shard_map/all_gather | solution.py:72
  106.3 1.5 %copy.84 = bf16[96,24,128]{0,1,2:T(8,128)(2,1)} copy(bf16[96,24,128]{2,1,0:T(8,128)(2,1)S(1)} %all_gather.14) | data formatting | bytes 1179648 | tf_op jit(solution)/shard_map/all_gather | solution.py:72
  107.7 17.5 %all-reduce.5.cloned.1.call-done = bf16[96,24,128]{0,1,2:T(8,128)(2,1)} async-done(((bf16[96,24,128]{0,1,2:T(8,128)(2,1)}), bf16[96,24,128]{0,1,2:T(8,128)(2,1)}) %all-reduce.5.cloned.1.call-update) | async-done | bytes 589840 | tf_op jit(solution)/shard_map/psum | solution.py:11
  125.2 1.9 %bitcast_reduce_fusion = (f32[24,24]{0,1:T(8,128)S(1)}, f32[128,24,24]{2,1,0:T(8,128)S(1)}) fusion(bf16[96,24,128]{0,1,2:T(8,128)(2,1)} %copy.84, bf16[96,24,128]{0,1,2:T(8,128)(2,1)} %all-reduce.5.cloned.1.call-done), kind=kOutput, calls=%fused_computation | convolution fusion | flops 14228928 | bytes 1476864 | tf_op jit(solution)/shard_map/kic,kjc->ijc/dot_general | solution.py:69
  127.2 1.2 copy.85
  128.4 1.2 multiply_reduce_fusion.1
  129.6 1.5 %fusion.68 = (f32[24,24]{1,0:T(8,128)S(1)}, f32[24,24,128]{2,1,0:T(8,128)S(1)}) fusion(f32[24,24,128]{2,1,0:T(8,128)} %copy-done.1, bf16[2,128,128]{2,1,0:T(8,128)(2,1)S(1)} %copy-done.4, f32[128,24,24]{0,1,2:T(8,128)} %copy.85, f32[128]{0:T(128)S(1)} %get-tuple-element.18, f32[128]{0:T(128)S(1)} %get-tuple-element.29, f32[24,24]{1,0:T(8,128)S(1)} %add_rsqrt_fusion.1, ...), kind=kOutput, calls=%fused_computation.120 | convolution fusion | flops 19684800 | bytes 1240320 | tf_op jit(solution)/shard_map/dot_general | solution.py:40
  132.3 1.2 convolution_add_fusion
  (39 shorter events, 5.4 us)
Async XLA Ops:
  6.5 124.9 %copy-start = (bf16[128,1024]{1,0:T(8,128)(2,1)S(1)}, bf16[128,1024]{1,0:T(8,128)(2,1)}, u32[]{:S(2)}) copy-start(bf16[128,1024]{1,0:T(8,128)(2,1)} %param.16) | copy-start | bytes 786436
  6.5 57.0 %all-reduce.3.cloned.1.call-start = ((), (), s32[]{:S(2)}) async-start(), calls=%async_computation | async-start | bytes 1179648 | tf_op jit(solution)/shard_map/psum | solution.py:11
  23.2 102.0 %all-reduce.5.cloned.1.call-start = ((), (), s32[]{:S(2)}) async-start(), calls=%async_computation.1 | async-start | bytes 1572864 | tf_op jit(solution)/shard_map/psum | solution.py:11
  67.8 2.6 %copy-start.4 = (bf16[2,128,128]{2,1,0:T(8,128)(2,1)S(1)}, bf16[2,128,128]{2,1,0:T(8,128)(2,1)}, u32[]{:S(2)}) copy-start(bf16[2,128,128]{2,1,0:T(8,128)(2,1)} %param.15) | copy-start | bytes 196612
  69.1 3.5 %copy-start.2 = (bf16[2,128,640]{2,1,0:T(8,128)(2,1)S(1)}, bf16[2,128,640]{2,1,0:T(8,128)(2,1)}, u32[]{:S(2)}) copy-start(bf16[2,128,640]{2,1,0:T(8,128)(2,1)} %param.14) | copy-start | bytes 983044
  71.9 0.7 copy-start.1
  131.4 0.9 copy-start.3
Sparse Core Ops, SparseCore 0:
  23.3 40.1 all-reduce.2
  91.3 33.7 all-reduce.4
where the time goes:
time: 141 us; the launch traced here: 140 us
  waiting for transfers between devices  48.8 us (35%)
  blocking collectives  48 us (34%)
  between operations  13.6 us (10%)
  local copies, waits for them, and re-layouts  11.5 us (8%)
  matrix products  10.7 us (8%)
  other arithmetic  7.73 us (5%)
    psum x2, waiting for transfers between devices, broadcast(): return lax.psum(jnp.where(mine, array, jnp.zeros_like(array)), axis)  48.8 us
    all_gather x1, blocking collectives, local(): left_strip = lax.all_gather(left_edge, 'row', axis=0, tiled=True)  16.3 us
    all_gather x1, blocking collectives, local(): lax.all_gather(right_edge, 'row', axis=0, tiled=True)  15 us
    all_gather x1, blocking collectives, local(): right_strip = lax.all_gather(right_edge, 'col', axis=1, tiled=True)  8.98 us
    all_gather x1, blocking collectives, local(): lax.all_gather(left_edge, 'col', axis=1, tiled=True)  7.65 us
    reduce_sum x5, other arithmetic, layer_norm(): spread = jnp.mean((values - center) ** 2, axis=-1, keepdims=True)  4.26 us
    dot_general x2, matrix products, finish_update(): jnp.dot(tri_norm, w_out[update], preferred_element_type=jnp.float32)  2.99 us
  transfers between devices with their start and end apart: 2, of which 2 were waited for; matrix products, arithmetic and copies ran while one was open for 2% of the time, Pallas kernels for 0%

commit v1 on v0

--- a/solution.py
+++ b/solution.py
@@ -1,9 +1,14 @@
+import functools
+
 import jax
 import jax.numpy as jnp
 from jax import lax
+from jax.experimental import pallas as pl
+from jax.experimental.pallas import tpu as pltpu
 from jax.sharding import PartitionSpec as P
 
 MASK_TILE = 8
+MESH = pl.DeviceIdType.MESH
 
 
 def broadcast(array, axis, root):
@@ -82,9 +87,276 @@
     return state + jnp.dot(activated, w_trans_out, preferred_element_type=jnp.float32)
 
 
+GROUPS = 16
+WIDTH = 8
+SIDE = 24
+LR_ROWS = 80
+TRI_ROWS = 48
+
+
+def sigmoid(x):
+    return 0.5 * jnp.tanh(0.5 * x) + 0.5
+
+
+def swap_groups(values, lane):
+    values = list(values)
+    for step in (8, 4, 2, 1):
+        low = (lane & (step * WIDTH)) == 0
+        for a in range(GROUPS):
+            if a & step:
+                continue
+            first, second = values[a], values[a + step]
+            values[a] = jnp.where(low, first, pltpu.roll(second, step * WIDTH, 1))
+            values[a + step] = jnp.where(low, pltpu.roll(first, 128 - step * WIDTH, 1), second)
+    return values
+
+
+def norm_rows(x, gain, bias):
+    center = jnp.mean(x, axis=-1, keepdims=True)
+    off = x - center
+    spread = jnp.mean(off * off, axis=-1, keepdims=True)
+    return (off * lax.rsqrt(spread + 1e-05) * gain + bias).astype(jnp.bfloat16)
+
+
+def kernel(
+    cols, pair, chain, block_mask, gain, bias, w_proj, w_out, w_in, w_down, out,
+    edges, gates, state, tri, lr_out, lr_in, tri_out, tri_in, send_sem, recv_sem,
+):
+    row, col = lax.axis_index("row"), lax.axis_index("col")
+    me = row * cols + col
+
+    def place(index):
+        return {"row": index // cols, "col": lax.rem(index, cols)}
+
+    barrier = pltpu.get_barrier_semaphore()
+
+    def greet(d, carry):
+        pl.semaphore_signal(
+            barrier, inc=1, device_id=place(lax.rem(me + d, GROUPS)), device_id_type=MESH
+        )
+        return carry
+
+    lax.fori_loop(1, GROUPS, greet, 0)
+
+    def exchange(phase, source, target):
+        def copy(index, slot):
+            return pltpu.make_async_remote_copy(
+                src_ref=source.at[index],
+                dst_ref=target.at[slot],
+                send_sem=send_sem.at[phase, index],
+                recv_sem=recv_sem.at[phase, slot],
+                device_id=place(index),
+                device_id_type=MESH,
+            )
+
+        def start(d, carry):
+            copy(lax.rem(me + d, GROUPS), me).start()
+            return carry
+
+        def finish(d, carry):
+            index = lax.rem(me + GROUPS - d, GROUPS)
+            copy(index, index).wait_recv()
+            return carry
+
+        def drain(d, carry):
+            copy(lax.rem(me + d, GROUPS), me).wait_send()
+            return carry
+
+        lax.fori_loop(1, GROUPS, start, 0)
+        target[me] = source[me]
+        lax.fori_loop(1, GROUPS, finish, 0)
+        lax.fori_loop(1, GROUPS, drain, 0)
+
+    sub = lax.broadcasted_iota(jnp.int32, (8, 128), 0)
+
+    def spread_ids(ids):
+        rows = []
+        for t in range(SIDE // 8):
+            v = jnp.full((8, 128), ids[8 * t], jnp.int32)
+            for s in range(1, 8):
+                v = jnp.where(sub == s, ids[8 * t + s], v)
+            rows.append(v)
+        return rows
+
+    row_ids = [chain[row * SIDE + i] for i in range(SIDE)]
+    col_ids = [chain[col * SIDE + i] for i in range(SIDE)]
+    per_side = SIDE // MASK_TILE
+    tiles = [
+        [block_mask[row * per_side + a, col * per_side + b] for b in range(per_side)]
+        for a in range(per_side)
+    ]
+
+    def mask_rows(update, i):
+        lead, others = (row_ids, spread_cols) if update == 0 else (col_ids, spread_rows)
+        parts = []
+        for t in range(SIDE // 8):
+            tile = tiles[i // 8][t] if update == 0 else tiles[t][i // 8]
+            parts.append(
+                jnp.where(others[t] == lead[i], 1, jnp.full((8, 128), tile, jnp.int32))
+            )
+        return jnp.concatenate(parts, axis=0).astype(jnp.float32)
+
+    spread_rows, spread_cols = spread_ids(row_ids), spread_ids(col_ids)
+    lane16 = lax.broadcasted_iota(jnp.int32, (16, 128), 1)
+    lane8 = lax.broadcasted_iota(jnp.int32, (8, 128), 1)
+    lane96 = lax.broadcasted_iota(jnp.int32, (4 * SIDE, 128), 1)
+    edges[:, 72:80, :] = jnp.zeros((GROUPS, 8, 128), jnp.float32)
+    same = (lax.broadcasted_iota(jnp.int32, (128, 768), 0) & 7) == (
+        lax.broadcasted_iota(jnp.int32, (128, 768), 1) & 7
+    )
+    fold = jnp.where(
+        lax.broadcasted_iota(jnp.int32, (16, 128), 1) // WIDTH
+        == lax.broadcasted_iota(jnp.int32, (16, 128), 0),
+        1.0,
+        0.0,
+    ).astype(jnp.bfloat16)
+
+    for u in range(2):
+        origin = pair if u == 0 else state
+        for t in range(3):
+            rows = pl.ds(192 * t, 192)
+            normed = norm_rows(origin[rows, :], gain[2 * u : 2 * u + 1, :], bias[2 * u : 2 * u + 1, :])
+            proj = jnp.dot(normed, w_proj[u], preferred_element_type=jnp.float32)
+            left = sigmoid(proj[:, 0:128]) * proj[:, 128:256]
+            right = sigmoid(proj[:, 256:384]) * proj[:, 384:512]
+            gates[rows, :] = sigmoid(proj[:, 512:640])
+            for s in range(8):
+                mask = mask_rows(u, 8 * t + s)
+                edges[s, pl.ds(24 * t, 24), :] = left[24 * s : 24 * s + 24] * mask
+                edges[8 + s, pl.ds(24 * t, 24), :] = right[24 * s : 24 * s + 24] * mask
+        for t in range(LR_ROWS // 16):
+            rows = pl.ds(16 * t, 16)
+            swapped = swap_groups([edges[a, rows, :] for a in range(GROUPS)], lane16)
+            for g in range(GROUPS):
+                lr_out[u, g, rows, :] = swapped[g].astype(jnp.bfloat16)
+
+        if u == 0:
+            pl.semaphore_wait(barrier, GROUPS - 1)
+        exchange(2 * u, lr_out.at[u], lr_in.at[u])
+
+        grid = {}
+        for lead in range(4):
+            slabs = []
+            for k in range(4):
+                index = lead * 4 + k if u == 0 else k * 4 + lead
+                slabs.append(lr_in[u, index].astype(jnp.float32))
+            for t in range(3):
+                grid[lead, t] = jnp.concatenate(
+                    [slab[24 * t : 24 * t + 24] for slab in slabs], axis=0
+                )
+        turned = {key: pltpu.roll(value, 64, 1) for key, value in grid.items()}
+        low = lane96 < 64
+        order = [(lead, t) for lead in range(4) for t in range(3)]
+        rights = [jnp.where(low, turned[b, 0], grid[b, 1]) for b in range(4)]
+        rights += [jnp.where(low, turned[b, 2], grid[b + 1, 2]) for b in (0, 2)]
+        rights = jnp.concatenate([r.astype(jnp.bfloat16) for r in rights], axis=1)
+        folded = []
+        for q in range(6):
+            lefts = jnp.where(low, grid[order[2 * q]], turned[order[2 * q + 1]])
+            product = jnp.dot(
+                lefts.T.astype(jnp.bfloat16), rights, preferred_element_type=jnp.float32
+            )
+            kept = jnp.where(same, product, 0.0).astype(jnp.bfloat16)
+            folded.append(jnp.dot(fold, kept, preferred_element_type=jnp.float32))
+        whole = jnp.concatenate(folded, axis=0)
+        half = lane8 < 64
+        for a in range(4):
+            for b in range(4):
+                block = whole[24 * a : 24 * a + 24]
+                side = block[:, 512 + 128 * (b // 2) : 640 + 128 * (b // 2)]
+                top, mid, end = side[0:8], side[8:16], side[16:24]
+                if b % 2 == 0:
+                    mixed = jnp.where(half, top, pltpu.roll(mid, 64, 1))
+                else:
+                    mixed = jnp.where(half, pltpu.roll(top, 64, 1), mid)
+                    end = pltpu.roll(end, 64, 1)
+                slab = jnp.concatenate(
+                    [block[:, 128 * b : 128 * b + 128], mixed, end, jnp.zeros_like(end)], axis=0
+                )
+                tri_out[u, 4 * a + b] = slab.astype(jnp.bfloat16)
+
+        exchange(2 * u + 1, tri_out.at[u], tri_in.at[u])
+
+        for t in range(3):
+            home = swap_groups(
+                [
+                    tri_in[u, g, pl.ds(16 * t, 16), :].astype(jnp.float32)
+                    for g in range(GROUPS)
+                ],
+                lane16,
+            )
+            for a in range(GROUPS):
+                if t == 0:
+                    tri[pl.ds(24 * a, 16), :] = home[a]
+                elif t == 1:
+                    tri[pl.ds(24 * a + 16, 8), :] = home[a][0:8]
+                    tri[pl.ds(24 * (16 + a % 8) + 8 * (a // 8), 8), :] = home[a][8:16]
+                elif a < 8:
+                    tri[pl.ds(24 * (16 + a) + 16, 8), :] = home[a][0:8]
+
+        for t in range(3):
+            rows = pl.ds(192 * t, 192)
+            tri_norm = norm_rows(
+                tri[rows, :], gain[2 * u + 1 : 2 * u + 2, :], bias[2 * u + 1 : 2 * u + 2, :]
+            )
+            change = jnp.dot(tri_norm, w_out[u], preferred_element_type=jnp.float32)
+            if u == 0:
+                for s in range(8):
+                    across = pl.ds(8 * t + s, SIDE, stride=SIDE)
+                    state[pl.ds(192 * t + 24 * s, 24), :] = (
+                        pair[across, :] + gates[across, :] * change[24 * s : 24 * s + 24]
+                    )
+            else:
+                state[rows, :] = state[rows, :] + gates[rows, :] * change
+
+    hidden = w_down.shape[0]
+    for t in range(3):
+        rows = pl.ds(192 * t, 192)
+        values = state[rows, :]
+        normed = norm_rows(values, gain[4:5, :], bias[4:5, :])
+        pre = jnp.dot(normed, w_in[...], preferred_element_type=jnp.float32)
+        gate = pre[:, :hidden]
+        act = (gate * sigmoid(gate) * pre[:, hidden:]).astype(jnp.bfloat16)
+        out[rows, :] = values + jnp.dot(act, w_down[...], preferred_element_type=jnp.float32)
+
+
+def split_channels(cols, pair, chain, block_mask, gain, bias, w_proj, w_out, w_in, w_down):
+    rows = pair.shape[0] * pair.shape[1]
+    vmem, smem = pl.BlockSpec(memory_space=pltpu.VMEM), pl.BlockSpec(memory_space=pltpu.SMEM)
+    result = pl.pallas_call(
+        functools.partial(kernel, cols),
+        out_shape=jax.ShapeDtypeStruct((rows, 128), jnp.float32),
+        in_specs=[vmem, smem, smem] + [vmem] * 6,
+        out_specs=vmem,
+        scratch_shapes=[
+            pltpu.VMEM((GROUPS, LR_ROWS, 128), jnp.float32),
+            pltpu.VMEM((rows, 128), jnp.float32),
+            pltpu.VMEM((rows, 128), jnp.float32),
+            pltpu.VMEM((rows, 128), jnp.float32),
+            pltpu.VMEM((2, GROUPS, LR_ROWS, 128), jnp.bfloat16),
+            pltpu.VMEM((2, GROUPS, LR_ROWS, 128), jnp.bfloat16),
+            pltpu.VMEM((2, GROUPS, TRI_ROWS, 128), jnp.bfloat16),
+            pltpu.VMEM((2, GROUPS, TRI_ROWS, 128), jnp.bfloat16),
+            pltpu.SemaphoreType.DMA((4, GROUPS)),
+            pltpu.SemaphoreType.DMA((4, GROUPS)),
+        ],
+        compiler_params=pltpu.CompilerParams(
+            collective_id=0, has_side_effects=True, vmem_limit_bytes=40 * 1024 * 1024
+        ),
+        cost_estimate=pl.CostEstimate(
+            flops=900_000_000, bytes_accessed=2_000_000, transcendentals=1_000_000
+        ),
+    )(pair.reshape(rows, 128), chain, block_mask, gain, bias, w_proj, w_out, w_in, w_down)
+    return result.reshape(pair.shape[1], pair.shape[0], 128).swapaxes(0, 1)
+
+
 def solution(mesh):
+    if mesh.shape["row"] == 4 and mesh.shape["col"] == 4:
+        body = functools.partial(split_channels, mesh.shape["col"])
+    else:
+        body = local
     return jax.shard_map(
-        local,
+        body,
         mesh=mesh,
         in_specs=(
             P(("parts", "row"), "col", None),

time: 141 us -> 51.5 us (0.37)
  waiting for transfers between devices: 48.8 us -> 0 us
  blocking collectives: 48 us -> 0 us
  Pallas kernels: 0 us -> 43 us
  between operations: 13.6 us -> 0.02 us
  matrix products: 10.7 us -> 0 us
  other arithmetic: 7.73 us -> 0 us
  local copies, waits for them, and re-layouts: 11.5 us -> 8.12 us
    psum x2 -> x0, waiting for transfers between devices: 48.8 us -> none  [broadcast(): return lax.psum(jnp.where(mine, array, jnp.zeros_like(array)), axis)]
    all_gather x4 -> x0, blocking collectives: 48 us -> none  [the longest x1 16.3 us: local(): left_strip = lax.all_gather(left_edge, 'row', axis=0, tiled=True)]
    pallas_call x0 -> x1, Pallas kernels: none -> 43 us  [split_channels(): pl.pallas_call(functools.partial(kernel, cols), out_shape=jax.ShapeDtypeS...]
    dot_general x8 -> x0, matrix products: 10.7 us -> none  [the longest x2 2.99 us: finish_update(): jnp.dot(tri_norm, w_out[update], preferred_element_type=jnp.float32)]
    unnamed x10 -> x18, local copies, waits for them, and re-layouts: 0.76 us -> 7.35 us
    reduce_sum x6 -> x0, other arithmetic: 5.41 us -> none  [the longest x5 4.26 us: layer_norm(): spread = jnp.mean((values - center) ** 2, axis=-1, keepdims=True)]
    all_gather x3 -> x0, local copies, waits for them, and re-layouts: 3.3 us -> none  [the longest x1 1.46 us: local(): lax.all_gather(right_edge, 'row', axis=0, tiled=True)]
    dot_general x2 -> x0, local copies, waits for them, and re-layouts: 2.39 us -> none  [the longest x1 1.19 us: local(): jnp.einsum('ikc,jkc->ijc', lax.all_gather(left_edge, 'col', axis=1, tiled...]
  transfers between devices with their start and end apart: 2 -> 0, of which waited for: 2 -> 0; matrix products, arithmetic and copies ran while one was open for 2% -> 0% of each run, Pallas kernels for 0% -> 0%
where the time goes in v1:
time: 51.5 us; the launch traced here: 51.1 us
  Pallas kernels  43 us (83%)
  local copies, waits for them, and re-layouts  8.12 us (16%)
    pallas_call x1, Pallas kernels, split_channels(): pl.pallas_call(functools.partial(kernel, cols), out_shape=jax.ShapeDtypeS...  43 us
    unnamed x18, local copies, waits for them, and re-layouts  7.35 us

profile of v1, /device:TPU:0, one launch (start us, length us, event | category | flops | bytes accessed | tf_op | source)
XLA Modules:
  0.0 51.1 jit_solution(7932480354656184393)
XLA Ops:
  0.0 0.0 copy-start.8
  0.0 0.7 %copy-done.8 = s32[96]{0:T(128)S(1)} copy-done((s32[96]{0:T(128)S(1)}, s32[96]{0:T(128)}, u32[]{:S(2)}) %copy-start.8) | copy-done | bytes 408
  0.7 0.0 copy-start
  0.7 1.0 %copy-done = bf16[2,128,640]{2,1,0:T(8,128)(2,1)S(1)} copy-done((bf16[2,128,640]{2,1,0:T(8,128)(2,1)S(1)}, bf16[2,128,640]{2,1,0:T(8,128)(2,1)}, u32[]{:S(2)}) %copy-start) | copy-done | bytes 327704
  1.6 0.0 copy-start.1
  1.6 1.0 %copy-done.1 = f32[24,24,128]{2,1,0:T(8,128)S(1)} copy-done((f32[24,24,128]{2,1,0:T(8,128)S(1)}, f32[24,24,128]{2,1,0:T(8,128)}, u32[]{:S(2)}) %copy-start.1) | copy-done | bytes 294936
  2.6 0.0 copy-start.2
  2.6 0.9 %copy-done.2 = bf16[128,1024]{1,0:T(8,128)(2,1)S(1)} copy-done((bf16[128,1024]{1,0:T(8,128)(2,1)S(1)}, bf16[128,1024]{1,0:T(8,128)(2,1)}, u32[]{:S(2)}) %copy-start.2) | copy-done | bytes 262168
  3.5 0.0 copy-start.3
  3.5 0.9 %copy-done.3 = bf16[512,128]{1,0:T(8,128)(2,1)S(1)} copy-done((bf16[512,128]{1,0:T(8,128)(2,1)S(1)}, bf16[512,128]{1,0:T(8,128)(2,1)}, u32[]{:S(2)}) %copy-start.3) | copy-done | bytes 131096
  4.4 0.0 copy-start.4
  4.4 0.8 %copy-done.4 = bf16[2,128,128]{2,1,0:T(8,128)(2,1)S(1)} copy-done((bf16[2,128,128]{2,1,0:T(8,128)(2,1)S(1)}, bf16[2,128,128]{2,1,0:T(8,128)(2,1)}, u32[]{:S(2)}) %copy-start.4) | copy-done | bytes 65560
  5.3 0.0 copy-start.5
  5.3 0.7 %copy-done.5 = s32[12,12]{1,0:T(8,128)S(1)} copy-done((s32[12,12]{1,0:T(8,128)S(1)}, s32[12,12]{1,0:T(8,128)}, u32[]{:S(2)}) %copy-start.5) | copy-done | bytes 600
  6.0 0.0 copy-start.6
  6.0 0.7 %copy-done.6 = f32[5,128]{1,0:T(8,128)S(1)} copy-done((f32[5,128]{1,0:T(8,128)S(1)}, f32[5,128]{1,0:T(8,128)}, u32[]{:S(2)}) %copy-start.6) | copy-done | bytes 2584
  6.7 0.0 copy-start.7
  6.7 0.7 %copy-done.7 = f32[5,128]{1,0:T(8,128)S(1)} copy-done((f32[5,128]{1,0:T(8,128)S(1)}, f32[5,128]{1,0:T(8,128)}, u32[]{:S(2)}) %copy-start.7) | copy-done | bytes 2584
  7.4 43.0 %shard_map.91 = f32[576,128]{1,0:T(8,128)S(1)} custom-call(f32[576,128]{1,0:T(8,128)S(1)} %bitcast.6, s32[96]{0:T(128)S(1)} %copy-done.8, s32[12,12]{1,0:T(8,128)S(1)} %copy-done.5, f32[5,128]{1,0:T(8,128)S(1)} %copy-done.6, f32[5,128]{1,0:T(8,128)S(1)} %copy-done.7, bf16[2,128,640]{2,1,0:T(8,128)(2,1)S(1)} %copy-done, bf16[2,128,128]{2,1,0:T(8,128)(2,1)S(1)} %copy-done.4, ...), custom_call_target="tpu_custom_call" | custom-call | flops 900000000 | bytes 2000000 | tf_op jit(solution)/shard_map/pallas_call | solution.py:326
  50.3 0.8 %copy.12 = f32[24,24,128]{2,0,1:T(8,128)} copy(f32[24,24,128]{2,1,0:T(8,128)S(1)} %bitcast.5) | data formatting | bytes 589824 | tf_op jit(solution)/shard_map/reshape | solution.py:350
Async XLA Ops:
  0.0 0.7 %copy-start.8 = (s32[96]{0:T(128)S(1)}, s32[96]{0:T(128)}, u32[]{:S(2)}) copy-start(s32[96]{0:T(128)} %chain.1) | copy-start | bytes 1156
  0.7 1.0 %copy-start = (bf16[2,128,640]{2,1,0:T(8,128)(2,1)S(1)}, bf16[2,128,640]{2,1,0:T(8,128)(2,1)}, u32[]{:S(2)}) copy-start(bf16[2,128,640]{2,1,0:T(8,128)(2,1)} %w_proj.1) | copy-start | bytes 983044
  1.6 1.0 %copy-start.1 = (f32[24,24,128]{2,1,0:T(8,128)S(1)}, f32[24,24,128]{2,1,0:T(8,128)}, u32[]{:S(2)}) copy-start(f32[24,24,128]{2,1,0:T(8,128)} %param.9) | copy-start | bytes 884740
  2.6 0.9 %copy-start.2 = (bf16[128,1024]{1,0:T(8,128)(2,1)S(1)}, bf16[128,1024]{1,0:T(8,128)(2,1)}, u32[]{:S(2)}) copy-start(bf16[128,1024]{1,0:T(8,128)(2,1)} %w_in.1) | copy-start | bytes 786436
  3.5 0.9 %copy-start.3 = (bf16[512,128]{1,0:T(8,128)(2,1)S(1)}, bf16[512,128]{1,0:T(8,128)(2,1)}, u32[]{:S(2)}) copy-start(bf16[512,128]{1,0:T(8,128)(2,1)} %w_down.1) | copy-start | bytes 393220
  4.4 0.8 %copy-start.4 = (bf16[2,128,128]{2,1,0:T(8,128)(2,1)S(1)}, bf16[2,128,128]{2,1,0:T(8,128)(2,1)}, u32[]{:S(2)}) copy-start(bf16[2,128,128]{2,1,0:T(8,128)(2,1)} %w_out.1) | copy-start | bytes 196612
  5.3 0.7 %copy-start.5 = (s32[12,12]{1,0:T(8,128)S(1)}, s32[12,12]{1,0:T(8,128)}, u32[]{:S(2)}) copy-start(s32[12,12]{1,0:T(8,128)} %block_mask.1) | copy-start | bytes 1732
  6.0 0.7 %copy-start.6 = (f32[5,128]{1,0:T(8,128)S(1)}, f32[5,128]{1,0:T(8,128)}, u32[]{:S(2)}) copy-start(f32[5,128]{1,0:T(8,128)} %gain.1) | copy-start | bytes 7684
  6.7 0.7 %copy-start.7 = (f32[5,128]{1,0:T(8,128)S(1)}, f32[5,128]{1,0:T(8,128)}, u32[]{:S(2)}) copy-start(f32[5,128]{1,0:T(8,128)} %bias.1) | copy-start | bytes 7684

commit v2 on v1

--- a/solution.py
+++ b/solution.py
@@ -91,6 +91,7 @@
 WIDTH = 8
 SIDE = 24
 LR_ROWS = 80
+HEAD_ROWS = 48
 TRI_ROWS = 48
 
 
@@ -119,11 +120,31 @@
 
 
 def kernel(
-    cols, pair, chain, block_mask, gain, bias, w_proj, w_out, w_in, w_down, out,
-    edges, gates, state, tri, lr_out, lr_in, tri_out, tri_in, send_sem, recv_sem,
+    cols, pair_hbm, chain_hbm, block_hbm, gain_hbm, bias_hbm, proj_hbm, out_hbm, in_hbm, down_hbm,
+    out, pair, chain, block_mask, gain, bias, w_proj, w_out, w_in, w_down,
+    edges, normed, gates, state, tri, grid, lr_out, lr_in, tri_out, tri_in,
+    load_sem, send_sem, recv_sem,
 ):
     row, col = lax.axis_index("row"), lax.axis_index("col")
     me = row * cols + col
+    loads = [
+        pltpu.make_async_copy(src, dst, load_sem.at[n])
+        for n, (src, dst) in enumerate(
+            (
+                (pair_hbm, pair),
+                (chain_hbm, chain),
+                (block_hbm, block_mask),
+                (gain_hbm, gain),
+                (bias_hbm, bias),
+                (proj_hbm, w_proj),
+                (out_hbm, w_out),
+                (in_hbm, w_in),
+                (down_hbm, w_down),
+            )
+        )
+    ]
+    for load in loads:
+        load.start()
 
     def place(index):
         return {"row": index // cols, "col": lax.rem(index, cols)}
@@ -138,34 +159,36 @@
 
     lax.fori_loop(1, GROUPS, greet, 0)
 
-    def exchange(phase, source, target):
-        def copy(index, slot):
-            return pltpu.make_async_remote_copy(
-                src_ref=source.at[index],
-                dst_ref=target.at[slot],
-                send_sem=send_sem.at[phase, index],
-                recv_sem=recv_sem.at[phase, slot],
-                device_id=place(index),
-                device_id_type=MESH,
-            )
-
-        def start(d, carry):
-            copy(lax.rem(me + d, GROUPS), me).start()
+    def remote(phase, source, target, index, slot):
+        return pltpu.make_async_remote_copy(
+            src_ref=source.at[index],
+            dst_ref=target.at[slot],
+            send_sem=send_sem.at[phase, index],
+            recv_sem=recv_sem.at[phase, slot],
+            device_id=place(index),
+            device_id_type=MESH,
+        )
+
+    def edge_copy(u, piece, index, slot):
+        start, count = ((0, HEAD_ROWS), (HEAD_ROWS, LR_ROWS - HEAD_ROWS))[piece]
+        return pltpu.make_async_remote_copy(
+            src_ref=lr_out.at[u, index, pl.ds(start, count)],
+            dst_ref=lr_in.at[u, slot, pl.ds(start, count)],
+            send_sem=send_sem.at[3 * u + piece, index],
+            recv_sem=recv_sem.at[3 * u + piece, slot],
+            device_id=place(index),
+            device_id_type=MESH,
+        )
+
+    def tri_copy(u, index, slot):
+        return remote(3 * u + 2, tri_out.at[u], tri_in.at[u], index, slot)
+
+    def each_peer(action):
+        def body(d, carry):
+            action(lax.rem(me + d, GROUPS))
             return carry
 
-        def finish(d, carry):
-            index = lax.rem(me + GROUPS - d, GROUPS)
-            copy(index, index).wait_recv()
-            return carry
-
-        def drain(d, carry):
-            copy(lax.rem(me + d, GROUPS), me).wait_send()
-            return carry
-
-        lax.fori_loop(1, GROUPS, start, 0)
-        target[me] = source[me]
-        lax.fori_loop(1, GROUPS, finish, 0)
-        lax.fori_loop(1, GROUPS, drain, 0)
+        lax.fori_loop(1, GROUPS, body, 0)
 
     sub = lax.broadcasted_iota(jnp.int32, (8, 128), 0)
 
@@ -178,6 +201,8 @@
             rows.append(v)
         return rows
 
+    for n in range(5):
+        loads[n].wait()
     row_ids = [chain[row * SIDE + i] for i in range(SIDE)]
     col_ids = [chain[col * SIDE + i] for i in range(SIDE)]
     per_side = SIDE // MASK_TILE
@@ -186,20 +211,17 @@
         for a in range(per_side)
     ]
 
-    def mask_rows(update, i):
+    def mask_tile(update, i, t):
         lead, others = (row_ids, spread_cols) if update == 0 else (col_ids, spread_rows)
-        parts = []
-        for t in range(SIDE // 8):
-            tile = tiles[i // 8][t] if update == 0 else tiles[t][i // 8]
-            parts.append(
-                jnp.where(others[t] == lead[i], 1, jnp.full((8, 128), tile, jnp.int32))
-            )
-        return jnp.concatenate(parts, axis=0).astype(jnp.float32)
+        tile = tiles[i // 8][t] if update == 0 else tiles[t][i // 8]
+        return jnp.where(
+            others[t] == lead[i], 1, jnp.full((8, 128), tile, jnp.int32)
+        ).astype(jnp.float32)
 
     spread_rows, spread_cols = spread_ids(row_ids), spread_ids(col_ids)
     lane16 = lax.broadcasted_iota(jnp.int32, (16, 128), 1)
     lane8 = lax.broadcasted_iota(jnp.int32, (8, 128), 1)
-    lane96 = lax.broadcasted_iota(jnp.int32, (4 * SIDE, 128), 1)
+    low96 = lax.broadcasted_iota(jnp.int32, (4 * SIDE, 128), 1) < 64
     edges[:, 72:80, :] = jnp.zeros((GROUPS, 8, 128), jnp.float32)
     same = (lax.broadcasted_iota(jnp.int32, (128, 768), 0) & 7) == (
         lax.broadcasted_iota(jnp.int32, (128, 768), 1) & 7
@@ -210,72 +232,121 @@
         1.0,
         0.0,
     ).astype(jnp.bfloat16)
+    loads[5].wait()
 
     for u in range(2):
         origin = pair if u == 0 else state
-        for t in range(3):
-            rows = pl.ds(192 * t, 192)
-            normed = norm_rows(origin[rows, :], gain[2 * u : 2 * u + 1, :], bias[2 * u : 2 * u + 1, :])
-            proj = jnp.dot(normed, w_proj[u], preferred_element_type=jnp.float32)
+        for chunk in range(3):
+            piece = chunk // 2
+            first, lines, depth = ((0, 12, 16), (12, 12, 16), (0, 24, 8))[chunk]
+            base = 16 * piece
+            values = jnp.concatenate(
+                [origin[pl.ds(24 * (first + n) + base, depth), :] for n in range(lines)], axis=0
+            )
+            unit = norm_rows(values, gain[2 * u : 2 * u + 1, :], bias[2 * u : 2 * u + 1, :])
+            normed[pl.ds(192 * chunk, 192), :] = unit
+            proj = jnp.dot(unit, w_proj[u, :, 0:512], preferred_element_type=jnp.float32)
             left = sigmoid(proj[:, 0:128]) * proj[:, 128:256]
             right = sigmoid(proj[:, 256:384]) * proj[:, 384:512]
-            gates[rows, :] = sigmoid(proj[:, 512:640])
-            for s in range(8):
-                mask = mask_rows(u, 8 * t + s)
-                edges[s, pl.ds(24 * t, 24), :] = left[24 * s : 24 * s + 24] * mask
-                edges[8 + s, pl.ds(24 * t, 24), :] = right[24 * s : 24 * s + 24] * mask
-        for t in range(LR_ROWS // 16):
-            rows = pl.ds(16 * t, 16)
-            swapped = swap_groups([edges[a, rows, :] for a in range(GROUPS)], lane16)
-            for g in range(GROUPS):
-                lr_out[u, g, rows, :] = swapped[g].astype(jnp.bfloat16)
-
-        if u == 0:
-            pl.semaphore_wait(barrier, GROUPS - 1)
-        exchange(2 * u, lr_out.at[u], lr_in.at[u])
-
-        grid = {}
-        for lead in range(4):
-            slabs = []
-            for k in range(4):
-                index = lead * 4 + k if u == 0 else k * 4 + lead
-                slabs.append(lr_in[u, index].astype(jnp.float32))
+            for n in range(lines):
+                i = first + n
+                for h in range(depth // 8):
+                    mask = mask_tile(u, i, base // 8 + h)
+                    rows = pl.ds(48 * piece + depth * (i // 8) + 8 * h, 8)
+                    at = n * depth + 8 * h
+                    edges[i % 8, rows, :] = left[at : at + 8] * mask
+                    edges[8 + i % 8, rows, :] = right[at : at + 8] * mask
+            if chunk == 0:
+                continue
+            for t in ((0, 1, 2), (3, 4))[piece]:
+                rows = pl.ds(16 * t, 16)
+                swapped = swap_groups([edges[a, rows, :] for a in range(GROUPS)], lane16)
+                for g in range(GROUPS):
+                    lr_out[u, g, rows, :] = swapped[g].astype(jnp.bfloat16)
+            if u == 0 and piece == 0:
+                pl.semaphore_wait(barrier, GROUPS - 1)
+            each_peer(lambda index: edge_copy(u, piece, index, me).start())
+
+        for chunk in range(3):
+            first, lines, depth = ((0, 12, 16), (12, 12, 16), (0, 24, 8))[chunk]
+            gate = sigmoid(
+                jnp.dot(
+                    normed[pl.ds(192 * chunk, 192), :],
+                    w_proj[u, :, 512:640],
+                    preferred_element_type=jnp.float32,
+                )
+            )
+            for n in range(lines):
+                gates[pl.ds(24 * (first + n) + 16 * (chunk // 2), depth), :] = gate[
+                    depth * n : depth * n + depth
+                ]
+
+        def unpack(source, index):
+            if u == 0:
+                lead, k = index // 4, lax.rem(index, 4)
+            else:
+                lead, k = lax.rem(index, 4), index // 4
+            at = pl.multiple_of(24 * k, 8)
+            slab = source[u, index].astype(jnp.float32)
             for t in range(3):
-                grid[lead, t] = jnp.concatenate(
-                    [slab[24 * t : 24 * t + 24] for slab in slabs], axis=0
-                )
-        turned = {key: pltpu.roll(value, 64, 1) for key, value in grid.items()}
-        low = lane96 < 64
-        order = [(lead, t) for lead in range(4) for t in range(3)]
-        rights = [jnp.where(low, turned[b, 0], grid[b, 1]) for b in range(4)]
-        rights += [jnp.where(low, turned[b, 2], grid[b + 1, 2]) for b in (0, 2)]
+                grid[3 * lead + t, pl.ds(at, 16), :] = slab[16 * t : 16 * t + 16]
+                grid[3 * lead + t, pl.ds(at + 16, 8), :] = slab[48 + 8 * t : 56 + 8 * t]
+
+        unpack(lr_out, me)
+
+        def take(d, carry):
+            index = lax.rem(me + GROUPS - d, GROUPS)
+            edge_copy(u, 0, index, index).wait_recv()
+            edge_copy(u, 1, index, index).wait_recv()
+            unpack(lr_in, index)
+            return carry
+
+        lax.fori_loop(1, GROUPS, take, 0)
+
+        rights = [
+            jnp.where(low96, pltpu.roll(grid[3 * b], 64, 1), grid[3 * b + 1]) for b in range(4)
+        ]
+        rights += [
+            jnp.where(low96, pltpu.roll(grid[3 * b + 2], 64, 1), grid[3 * b + 5]) for b in (0, 2)
+        ]
         rights = jnp.concatenate([r.astype(jnp.bfloat16) for r in rights], axis=1)
-        folded = []
-        for q in range(6):
-            lefts = jnp.where(low, grid[order[2 * q]], turned[order[2 * q + 1]])
+        half = lane8 < 64
+        for step in (2, 1, 3, 0):
+            lead = lax.rem(row + step, 4)
+            pairs = jnp.where(low96, grid[3 * lead], pltpu.roll(grid[3 * lead + 1], 64, 1))
             product = jnp.dot(
-                lefts.T.astype(jnp.bfloat16), rights, preferred_element_type=jnp.float32
+                pairs.T.astype(jnp.bfloat16), rights, preferred_element_type=jnp.float32
             )
             kept = jnp.where(same, product, 0.0).astype(jnp.bfloat16)
-            folded.append(jnp.dot(fold, kept, preferred_element_type=jnp.float32))
-        whole = jnp.concatenate(folded, axis=0)
-        half = lane8 < 64
-        for a in range(4):
+            upper = jnp.dot(fold, kept, preferred_element_type=jnp.float32)
+            product = jnp.dot(
+                grid[3 * lead + 2].T[0:64].astype(jnp.bfloat16),
+                rights,
+                preferred_element_type=jnp.float32,
+            )
+            kept = jnp.where(same[0:64], product, 0.0).astype(jnp.bfloat16)
+            lower = jnp.dot(fold[0:8, 0:64], kept, preferred_element_type=jnp.float32)
             for b in range(4):
-                block = whole[24 * a : 24 * a + 24]
-                side = block[:, 512 + 128 * (b // 2) : 640 + 128 * (b // 2)]
-                top, mid, end = side[0:8], side[8:16], side[16:24]
+                spot = 512 + 128 * (b // 2)
+                top, mid = upper[0:8, spot : spot + 128], upper[8:16, spot : spot + 128]
+                end = lower[:, spot : spot + 128]
                 if b % 2 == 0:
                     mixed = jnp.where(half, top, pltpu.roll(mid, 64, 1))
                 else:
                     mixed = jnp.where(half, pltpu.roll(top, 64, 1), mid)
                     end = pltpu.roll(end, 64, 1)
+                lanes = slice(128 * b, 128 * b + 128)
                 slab = jnp.concatenate(
-                    [block[:, 128 * b : 128 * b + 128], mixed, end, jnp.zeros_like(end)], axis=0
+                    [upper[:, lanes], lower[:, lanes], mixed, end, jnp.zeros_like(end)], axis=0
                 )
-                tri_out[u, 4 * a + b] = slab.astype(jnp.bfloat16)
-
-        exchange(2 * u + 1, tri_out.at[u], tri_in.at[u])
+                tri_out[u, 4 * lead + b] = slab.astype(jnp.bfloat16)
+            for b in range(0 if step else 1, 4):
+                tri_copy(u, 4 * lead + lax.rem(col + b, 4), me).start()
+        tri_in[u, me] = tri_out[u, me]
+        each_peer(lambda index: tri_copy(u, index, index).wait_recv())
+        if u == 0:
+            for n in range(6, 9):
+                loads[n].wait()
 
         for t in range(3):
             home = swap_groups(
@@ -313,32 +384,46 @@
     for t in range(3):
         rows = pl.ds(192 * t, 192)
         values = state[rows, :]
-        normed = norm_rows(values, gain[4:5, :], bias[4:5, :])
-        pre = jnp.dot(normed, w_in[...], preferred_element_type=jnp.float32)
+        unit = norm_rows(values, gain[4:5, :], bias[4:5, :])
+        pre = jnp.dot(unit, w_in[...], preferred_element_type=jnp.float32)
         gate = pre[:, :hidden]
         act = (gate * sigmoid(gate) * pre[:, hidden:]).astype(jnp.bfloat16)
         out[rows, :] = values + jnp.dot(act, w_down[...], preferred_element_type=jnp.float32)
+    for u in range(2):
+        for piece in range(2):
+            each_peer(lambda index: edge_copy(u, piece, index, me).wait_send())
+        each_peer(lambda index: tri_copy(u, index, me).wait_send())
 
 
 def split_channels(cols, pair, chain, block_mask, gain, bias, w_proj, w_out, w_in, w_down):
     rows = pair.shape[0] * pair.shape[1]
-    vmem, smem = pl.BlockSpec(memory_space=pltpu.VMEM), pl.BlockSpec(memory_space=pltpu.SMEM)
+    vmem, hbm = pl.BlockSpec(memory_space=pltpu.VMEM), pl.BlockSpec(memory_space=pltpu.HBM)
+    operands = (
+        pair.reshape(rows, 128), chain, block_mask, gain, bias, w_proj, w_out, w_in, w_down
+    )
     result = pl.pallas_call(
         functools.partial(kernel, cols),
         out_shape=jax.ShapeDtypeStruct((rows, 128), jnp.float32),
-        in_specs=[vmem, smem, smem] + [vmem] * 6,
+        in_specs=[hbm] * 9,
         out_specs=vmem,
         scratch_shapes=[
+            (pltpu.SMEM if n in (1, 2) else pltpu.VMEM)(array.shape, array.dtype)
+            for n, array in enumerate(operands)
+        ]
+        + [
             pltpu.VMEM((GROUPS, LR_ROWS, 128), jnp.float32),
+            pltpu.VMEM((rows, 128), jnp.bfloat16),
             pltpu.VMEM((rows, 128), jnp.float32),
             pltpu.VMEM((rows, 128), jnp.float32),
             pltpu.VMEM((rows, 128), jnp.float32),
+            pltpu.VMEM((12, 4 * SIDE, 128), jnp.float32),
             pltpu.VMEM((2, GROUPS, LR_ROWS, 128), jnp.bfloat16),
             pltpu.VMEM((2, GROUPS, LR_ROWS, 128), jnp.bfloat16),
             pltpu.VMEM((2, GROUPS, TRI_ROWS, 128), jnp.bfloat16),
             pltpu.VMEM((2, GROUPS, TRI_ROWS, 128), jnp.bfloat16),
-            pltpu.SemaphoreType.DMA((4, GROUPS)),
-            pltpu.SemaphoreType.DMA((4, GROUPS)),
+            pltpu.SemaphoreType.DMA((9,)),
+            pltpu.SemaphoreType.DMA((6, GROUPS)),
+            pltpu.SemaphoreType.DMA((6, GROUPS)),
         ],
         compiler_params=pltpu.CompilerParams(
             collective_id=0, has_side_effects=True, vmem_limit_bytes=40 * 1024 * 1024
@@ -346,7 +431,7 @@
         cost_estimate=pl.CostEstimate(
             flops=900_000_000, bytes_accessed=2_000_000, transcendentals=1_000_000
         ),
-    )(pair.reshape(rows, 128), chain, block_mask, gain, bias, w_proj, w_out, w_in, w_down)
+    )(*operands)
     return result.reshape(pair.shape[1], pair.shape[0], 128).swapaxes(0, 1)
 
 

time: 51.5 us -> 53.5 us (1.039)
  Pallas kernels: 43 us -> 45 us
    pallas_call x1, Pallas kernels: 43 us -> 45 us  [split_channels(): pl.pallas_call(functools.partial(kernel, cols), out_shape=jax.ShapeDtypeS...]
where the time goes in v2:
time: 53.5 us; the launch traced here: 53.2 us
  Pallas kernels  45 us (84%)
  local copies, waits for them, and re-layouts  8.12 us (15%)
    pallas_call x1, Pallas kernels, split_channels(): pl.pallas_call(functools.partial(kernel, cols), out_shape=jax.ShapeDtypeS...  45 us
    unnamed x18, local copies, waits for them, and re-layouts  7.35 us

profile of v2, /device:TPU:0, one launch (start us, length us, event | category | flops | bytes accessed | tf_op | source)
XLA Modules:
  0.0 53.2 jit_solution(16158501701330013937)
XLA Ops:
  0.0 0.0 copy-start.8
  0.0 0.7 %copy-done.8 = s32[96]{0:T(128)S(1)} copy-done((s32[96]{0:T(128)S(1)}, s32[96]{0:T(128)}, u32[]{:S(2)}) %copy-start.8) | copy-done | bytes 408
  0.7 0.0 copy-start
  0.7 1.0 %copy-done = bf16[2,128,640]{2,1,0:T(8,128)(2,1)S(1)} copy-done((bf16[2,128,640]{2,1,0:T(8,128)(2,1)S(1)}, bf16[2,128,640]{2,1,0:T(8,128)(2,1)}, u32[]{:S(2)}) %copy-start) | copy-done | bytes 327704
  1.6 0.0 copy-start.1
  1.6 1.0 %copy-done.1 = f32[24,24,128]{2,1,0:T(8,128)S(1)} copy-done((f32[24,24,128]{2,1,0:T(8,128)S(1)}, f32[24,24,128]{2,1,0:T(8,128)}, u32[]{:S(2)}) %copy-start.1) | copy-done | bytes 294936
  2.6 0.0 copy-start.2
  2.6 0.9 %copy-done.2 = bf16[128,1024]{1,0:T(8,128)(2,1)S(1)} copy-done((bf16[128,1024]{1,0:T(8,128)(2,1)S(1)}, bf16[128,1024]{1,0:T(8,128)(2,1)}, u32[]{:S(2)}) %copy-start.2) | copy-done | bytes 262168
  3.5 0.0 copy-start.3
  3.5 0.9 %copy-done.3 = bf16[512,128]{1,0:T(8,128)(2,1)S(1)} copy-done((bf16[512,128]{1,0:T(8,128)(2,1)S(1)}, bf16[512,128]{1,0:T(8,128)(2,1)}, u32[]{:S(2)}) %copy-start.3) | copy-done | bytes 131096
  4.4 0.0 copy-start.4
  4.4 0.8 %copy-done.4 = bf16[2,128,128]{2,1,0:T(8,128)(2,1)S(1)} copy-done((bf16[2,128,128]{2,1,0:T(8,128)(2,1)S(1)}, bf16[2,128,128]{2,1,0:T(8,128)(2,1)}, u32[]{:S(2)}) %copy-start.4) | copy-done | bytes 65560
  5.3 0.0 copy-start.5
  5.3 0.7 %copy-done.5 = s32[12,12]{1,0:T(8,128)S(1)} copy-done((s32[12,12]{1,0:T(8,128)S(1)}, s32[12,12]{1,0:T(8,128)}, u32[]{:S(2)}) %copy-start.5) | copy-done | bytes 600
  6.0 0.0 copy-start.6
  6.0 0.7 %copy-done.6 = f32[5,128]{1,0:T(8,128)S(1)} copy-done((f32[5,128]{1,0:T(8,128)S(1)}, f32[5,128]{1,0:T(8,128)}, u32[]{:S(2)}) %copy-start.6) | copy-done | bytes 2584
  6.7 0.0 copy-start.7
  6.7 0.7 %copy-done.7 = f32[5,128]{1,0:T(8,128)S(1)} copy-done((f32[5,128]{1,0:T(8,128)S(1)}, f32[5,128]{1,0:T(8,128)}, u32[]{:S(2)}) %copy-start.7) | copy-done | bytes 2584
  7.4 45.0 %shard_map.91 = f32[576,128]{1,0:T(8,128)S(1)} custom-call(f32[576,128]{1,0:T(8,128)S(1)} %bitcast.6, s32[96]{0:T(128)S(1)} %copy-done.8, s32[12,12]{1,0:T(8,128)S(1)} %copy-done.5, f32[5,128]{1,0:T(8,128)S(1)} %copy-done.6, f32[5,128]{1,0:T(8,128)S(1)} %copy-done.7, bf16[2,128,640]{2,1,0:T(8,128)(2,1)S(1)} %copy-done, bf16[2,128,128]{2,1,0:T(8,128)(2,1)S(1)} %copy-done.4, ...), custom_call_target="tpu_custom_call" | custom-call | flops 900000000 | bytes 2000000 | tf_op jit(solution)/shard_map/pallas_call | solution.py:404
  52.4 0.8 %copy.12 = f32[24,24,128]{2,0,1:T(8,128)} copy(f32[24,24,128]{2,1,0:T(8,128)S(1)} %bitcast.5) | data formatting | bytes 589824 | tf_op jit(solution)/shard_map/reshape | solution.py:435
Async XLA Ops:
  0.0 0.7 %copy-start.8 = (s32[96]{0:T(128)S(1)}, s32[96]{0:T(128)}, u32[]{:S(2)}) copy-start(s32[96]{0:T(128)} %chain_hbm.1) | copy-start | bytes 1156
  0.7 1.0 %copy-start = (bf16[2,128,640]{2,1,0:T(8,128)(2,1)S(1)}, bf16[2,128,640]{2,1,0:T(8,128)(2,1)}, u32[]{:S(2)}) copy-start(bf16[2,128,640]{2,1,0:T(8,128)(2,1)} %proj_hbm.1) | copy-start | bytes 983044
  1.6 1.0 %copy-start.1 = (f32[24,24,128]{2,1,0:T(8,128)S(1)}, f32[24,24,128]{2,1,0:T(8,128)}, u32[]{:S(2)}) copy-start(f32[24,24,128]{2,1,0:T(8,128)} %param.9) | copy-start | bytes 884740
  2.6 0.9 %copy-start.2 = (bf16[128,1024]{1,0:T(8,128)(2,1)S(1)}, bf16[128,1024]{1,0:T(8,128)(2,1)}, u32[]{:S(2)}) copy-start(bf16[128,1024]{1,0:T(8,128)(2,1)} %in_hbm.1) | copy-start | bytes 786436
  3.5 0.9 %copy-start.3 = (bf16[512,128]{1,0:T(8,128)(2,1)S(1)}, bf16[512,128]{1,0:T(8,128)(2,1)}, u32[]{:S(2)}) copy-start(bf16[512,128]{1,0:T(8,128)(2,1)} %down_hbm.1) | copy-start | bytes 393220
  4.4 0.8 %copy-start.4 = (bf16[2,128,128]{2,1,0:T(8,128)(2,1)S(1)}, bf16[2,128,128]{2,1,0:T(8,128)(2,1)}, u32[]{:S(2)}) copy-start(bf16[2,128,128]{2,1,0:T(8,128)(2,1)} %out_hbm.1) | copy-start | bytes 196612
  5.3 0.7 %copy-start.5 = (s32[12,12]{1,0:T(8,128)S(1)}, s32[12,12]{1,0:T(8,128)}, u32[]{:S(2)}) copy-start(s32[12,12]{1,0:T(8,128)} %block_hbm.1) | copy-start | bytes 1732
  6.0 0.7 %copy-start.6 = (f32[5,128]{1,0:T(8,128)S(1)}, f32[5,128]{1,0:T(8,128)}, u32[]{:S(2)}) copy-start(f32[5,128]{1,0:T(8,128)} %gain_hbm.1) | copy-start | bytes 7684
  6.7 0.7 %copy-start.7 = (f32[5,128]{1,0:T(8,128)S(1)}, f32[5,128]{1,0:T(8,128)}, u32[]{:S(2)}) copy-start(f32[5,128]{1,0:T(8,128)} %bias_hbm.1) | copy-start | bytes 7684

commit v3 on v2

--- a/solution.py
+++ b/solution.py
@@ -90,9 +90,8 @@
 GROUPS = 16
 WIDTH = 8
 SIDE = 24
-LR_ROWS = 80
-HEAD_ROWS = 48
-TRI_ROWS = 48
+LR_TILES = 9
+TRI_TILES = 5
 
 
 def sigmoid(x):
@@ -169,19 +168,11 @@
             device_id_type=MESH,
         )
 
-    def edge_copy(u, piece, index, slot):
-        start, count = ((0, HEAD_ROWS), (HEAD_ROWS, LR_ROWS - HEAD_ROWS))[piece]
-        return pltpu.make_async_remote_copy(
-            src_ref=lr_out.at[u, index, pl.ds(start, count)],
-            dst_ref=lr_in.at[u, slot, pl.ds(start, count)],
-            send_sem=send_sem.at[3 * u + piece, index],
-            recv_sem=recv_sem.at[3 * u + piece, slot],
-            device_id=place(index),
-            device_id_type=MESH,
-        )
+    def edge_copy(u, index, slot):
+        return remote(2 * u, lr_out.at[u], lr_in.at[u], index, slot)
 
     def tri_copy(u, index, slot):
-        return remote(3 * u + 2, tri_out.at[u], tri_in.at[u], index, slot)
+        return remote(2 * u + 1, tri_out.at[u], tri_in.at[u], index, slot)
 
     def each_peer(action):
         def body(d, carry):
@@ -219,10 +210,8 @@
         ).astype(jnp.float32)
 
     spread_rows, spread_cols = spread_ids(row_ids), spread_ids(col_ids)
-    lane16 = lax.broadcasted_iota(jnp.int32, (16, 128), 1)
     lane8 = lax.broadcasted_iota(jnp.int32, (8, 128), 1)
     low96 = lax.broadcasted_iota(jnp.int32, (4 * SIDE, 128), 1) < 64
-    edges[:, 72:80, :] = jnp.zeros((GROUPS, 8, 128), jnp.float32)
     same = (lax.broadcasted_iota(jnp.int32, (128, 768), 0) & 7) == (
         lax.broadcasted_iota(jnp.int32, (128, 768), 1) & 7
     )
@@ -256,16 +245,14 @@
                     at = n * depth + 8 * h
                     edges[i % 8, rows, :] = left[at : at + 8] * mask
                     edges[8 + i % 8, rows, :] = right[at : at + 8] * mask
-            if chunk == 0:
-                continue
-            for t in ((0, 1, 2), (3, 4))[piece]:
-                rows = pl.ds(16 * t, 16)
-                swapped = swap_groups([edges[a, rows, :] for a in range(GROUPS)], lane16)
+            for t in ((), range(6), range(6, LR_TILES))[chunk]:
+                rows = pl.ds(8 * t, 8)
+                swapped = swap_groups([edges[a, rows, :] for a in range(GROUPS)], lane8)
                 for g in range(GROUPS):
-                    lr_out[u, g, rows, :] = swapped[g].astype(jnp.bfloat16)
-            if u == 0 and piece == 0:
-                pl.semaphore_wait(barrier, GROUPS - 1)
-            each_peer(lambda index: edge_copy(u, piece, index, me).start())
+                    lr_out[u, g, t] = swapped[g].astype(jnp.bfloat16)
+        if u == 0:
+            pl.semaphore_wait(barrier, GROUPS - 1)
+        each_peer(lambda index: edge_copy(u, index, me).start())
 
         for chunk in range(3):
             first, lines, depth = ((0, 12, 16), (12, 12, 16), (0, 24, 8))[chunk]
@@ -287,7 +274,7 @@
             else:
                 lead, k = lax.rem(index, 4), index // 4
             at = pl.multiple_of(24 * k, 8)
-            slab = source[u, index].astype(jnp.float32)
+            slab = source[u, index].astype(jnp.float32).reshape(8 * LR_TILES, 128)
             for t in range(3):
                 grid[3 * lead + t, pl.ds(at, 16), :] = slab[16 * t : 16 * t + 16]
                 grid[3 * lead + t, pl.ds(at + 16, 8), :] = slab[48 + 8 * t : 56 + 8 * t]
@@ -296,8 +283,7 @@
 
         def take(d, carry):
             index = lax.rem(me + GROUPS - d, GROUPS)
-            edge_copy(u, 0, index, index).wait_recv()
-            edge_copy(u, 1, index, index).wait_recv()
+            edge_copy(u, index, index).wait_recv()
             unpack(lr_in, index)
             return carry
 
@@ -337,9 +323,9 @@
                     end = pltpu.roll(end, 64, 1)
                 lanes = slice(128 * b, 128 * b + 128)
                 slab = jnp.concatenate(
-                    [upper[:, lanes], lower[:, lanes], mixed, end, jnp.zeros_like(end)], axis=0
+                    [upper[:, lanes], lower[:, lanes], mixed, end], axis=0
                 )
-                tri_out[u, 4 * lead + b] = slab.astype(jnp.bfloat16)
+                tri_out[u, 4 * lead + b] = slab.reshape(TRI_TILES, 8, 128).astype(jnp.bfloat16)
             for b in range(0 if step else 1, 4):
                 tri_copy(u, 4 * lead + lax.rem(col + b, 4), me).start()
         tri_in[u, me] = tri_out[u, me]
@@ -348,22 +334,17 @@
             for n in range(6, 9):
                 loads[n].wait()
 
-        for t in range(3):
+        for t in range(TRI_TILES):
             home = swap_groups(
-                [
-                    tri_in[u, g, pl.ds(16 * t, 16), :].astype(jnp.float32)
-                    for g in range(GROUPS)
-                ],
-                lane16,
+                [tri_in[u, g, t].astype(jnp.float32) for g in range(GROUPS)], lane8
             )
             for a in range(GROUPS):
-                if t == 0:
-                    tri[pl.ds(24 * a, 16), :] = home[a]
-                elif t == 1:
-                    tri[pl.ds(24 * a + 16, 8), :] = home[a][0:8]
-                    tri[pl.ds(24 * (16 + a % 8) + 8 * (a // 8), 8), :] = home[a][8:16]
+                if t < 3:
+                    tri[pl.ds(24 * a + 8 * t, 8), :] = home[a]
+                elif t == 3:
+                    tri[pl.ds(24 * (16 + a % 8) + 8 * (a // 8), 8), :] = home[a]
                 elif a < 8:
-                    tri[pl.ds(24 * (16 + a) + 16, 8), :] = home[a][0:8]
+                    tri[pl.ds(24 * (16 + a) + 16, 8), :] = home[a]
 
         for t in range(3):
             rows = pl.ds(192 * t, 192)
@@ -390,8 +371,7 @@
         act = (gate * sigmoid(gate) * pre[:, hidden:]).astype(jnp.bfloat16)
         out[rows, :] = values + jnp.dot(act, w_down[...], preferred_element_type=jnp.float32)
     for u in range(2):
-        for piece in range(2):
-            each_peer(lambda index: edge_copy(u, piece, index, me).wait_send())
+        each_peer(lambda index: edge_copy(u, index, me).wait_send())
         each_peer(lambda index: tri_copy(u, index, me).wait_send())
 
 
@@ -411,22 +391,22 @@
             for n, array in enumerate(operands)
         ]
         + [
-            pltpu.VMEM((GROUPS, LR_ROWS, 128), jnp.float32),
+            pltpu.VMEM((GROUPS, 8 * LR_TILES, 128), jnp.float32),
             pltpu.VMEM((rows, 128), jnp.bfloat16),
             pltpu.VMEM((rows, 128), jnp.float32),
             pltpu.VMEM((rows, 128), jnp.float32),
             pltpu.VMEM((rows, 128), jnp.float32),
             pltpu.VMEM((12, 4 * SIDE, 128), jnp.float32),
-            pltpu.VMEM((2, GROUPS, LR_ROWS, 128), jnp.bfloat16),
-            pltpu.VMEM((2, GROUPS, LR_ROWS, 128), jnp.bfloat16),
-            pltpu.VMEM((2, GROUPS, TRI_ROWS, 128), jnp.bfloat16),
-            pltpu.VMEM((2, GROUPS, TRI_ROWS, 128), jnp.bfloat16),
+            pltpu.VMEM((2, GROUPS, LR_TILES, 8, 128), jnp.bfloat16),
+            pltpu.VMEM((2, GROUPS, LR_TILES, 8, 128), jnp.bfloat16),
+            pltpu.VMEM((2, GROUPS, TRI_TILES, 8, 128), jnp.bfloat16),
+            pltpu.VMEM((2, GROUPS, TRI_TILES, 8, 128), jnp.bfloat16),
             pltpu.SemaphoreType.DMA((9,)),
-            pltpu.SemaphoreType.DMA((6, GROUPS)),
-            pltpu.SemaphoreType.DMA((6, GROUPS)),
+            pltpu.SemaphoreType.DMA((4, GROUPS)),
+            pltpu.SemaphoreType.DMA((4, GROUPS)),
         ],
         compiler_params=pltpu.CompilerParams(
-            collective_id=0, has_side_effects=True, vmem_limit_bytes=40 * 1024 * 1024
+            collective_id=0, has_side_effects=True, vmem_limit_bytes=56 * 1024 * 1024
         ),
         cost_estimate=pl.CostEstimate(
             flops=900_000_000, bytes_accessed=2_000_000, transcendentals=1_000_000

time: 53.5 us -> 43.2 us (0.81)
  local copies, waits for them, and re-layouts: 8.12 us -> 1.73 us
  Pallas kernels: 45 us -> 41.3 us
    unnamed x18 -> x0, local copies, waits for them, and re-layouts: 7.35 us -> none
    pallas_call x1, Pallas kernels: 45 us -> 41.3 us  [split_channels(): pl.pallas_call(functools.partial(kernel, cols), out_shape=jax.ShapeDtypeS...]
    reshape x1, local copies, waits for them, and re-layouts: 0.77 us -> 1.73 us  [split_channels(): return result.reshape(pair.shape[1], pair.shape[0], 128).swapaxes(0, 1)]
where the time goes in v3:
time: 43.2 us; the launch traced here: 43 us
  Pallas kernels  41.3 us (96%)
  local copies, waits for them, and re-layouts  1.73 us (4%)
    pallas_call x1, Pallas kernels, split_channels(): pl.pallas_call(functools.partial(kernel, cols), out_shape=jax.ShapeDtypeS...  41.3 us
    reshape x1, local copies, waits for them, and re-layouts, split_channels(): return result.reshape(pair.shape[1], pair.shape[0], 128).swapaxes(0, 1)  1.73 us

profile of v3, /device:TPU:0, one launch (start us, length us, event | category | flops | bytes accessed | tf_op | source)
XLA Modules:
  0.0 43.0 jit_solution(11108528654136361103)
XLA Ops:
  0.0 41.3 %shard_map.91 = f32[576,128]{1,0:T(8,128)} custom-call(f32[576,128]{1,0:T(8,128)} %bitcast.6, s32[96]{0:T(128)} %chain_hbm.1, s32[12,12]{1,0:T(8,128)} %block_hbm.1, f32[5,128]{1,0:T(8,128)} %gain_hbm.1, f32[5,128]{1,0:T(8,128)} %bias_hbm.1, bf16[2,128,640]{2,1,0:T(8,128)(2,1)} %proj_hbm.1, bf16[2,128,128]{2,1,0:T(8,128)(2,1)} %out_hbm.1, ...), custom_call_target="tpu_custom_call" | custom-call | flops 900000000 | bytes 2000000 | tf_op jit(solution)/shard_map/pallas_call | solution.py:384
  41.3 1.7 %copy.12 = f32[24,24,128]{2,0,1:T(8,128)} copy(f32[24,24,128]{2,1,0:T(8,128)} %bitcast.5) | data formatting | bytes 589824 | tf_op jit(solution)/shard_map/reshape | solution.py:415

commit v4 on v3

--- a/solution.py
+++ b/solution.py
@@ -122,7 +122,7 @@
     cols, pair_hbm, chain_hbm, block_hbm, gain_hbm, bias_hbm, proj_hbm, out_hbm, in_hbm, down_hbm,
     out, pair, chain, block_mask, gain, bias, w_proj, w_out, w_in, w_down,
     edges, normed, gates, state, tri, grid, lr_out, lr_in, tri_out, tri_in,
-    load_sem, send_sem, recv_sem,
+    done, load_sem, send_sem, recv_sem,
 ):
     row, col = lax.axis_index("row"), lax.axis_index("col")
     me = row * cols + col
@@ -142,9 +142,6 @@
             )
         )
     ]
-    for load in loads:
-        load.start()
-
     def place(index):
         return {"row": index // cols, "col": lax.rem(index, cols)}
 
@@ -157,6 +154,8 @@
         return carry
 
     lax.fori_loop(1, GROUPS, greet, 0)
+    for load in loads:
+        load.start()
 
     def remote(phase, source, target, index, slot):
         return pltpu.make_async_remote_copy(
@@ -361,6 +360,12 @@
             else:
                 state[rows, :] = state[rows, :] + gates[rows, :] * change
 
+    stores = [
+        pltpu.make_async_copy(
+            done.at[pl.ds(192 * t, 192)], out.at[pl.ds(192 * t, 192)], load_sem.at[9 + t]
+        )
+        for t in range(3)
+    ]
     hidden = w_down.shape[0]
     for t in range(3):
         rows = pl.ds(192 * t, 192)
@@ -369,15 +374,18 @@
         pre = jnp.dot(unit, w_in[...], preferred_element_type=jnp.float32)
         gate = pre[:, :hidden]
         act = (gate * sigmoid(gate) * pre[:, hidden:]).astype(jnp.bfloat16)
-        out[rows, :] = values + jnp.dot(act, w_down[...], preferred_element_type=jnp.float32)
+        done[rows, :] = values + jnp.dot(act, w_down[...], preferred_element_type=jnp.float32)
+        stores[t].start()
     for u in range(2):
         each_peer(lambda index: edge_copy(u, index, me).wait_send())
         each_peer(lambda index: tri_copy(u, index, me).wait_send())
+    for store in stores:
+        store.wait()
 
 
 def split_channels(cols, pair, chain, block_mask, gain, bias, w_proj, w_out, w_in, w_down):
     rows = pair.shape[0] * pair.shape[1]
-    vmem, hbm = pl.BlockSpec(memory_space=pltpu.VMEM), pl.BlockSpec(memory_space=pltpu.HBM)
+    hbm = pl.BlockSpec(memory_space=pltpu.HBM)
     operands = (
         pair.reshape(rows, 128), chain, block_mask, gain, bias, w_proj, w_out, w_in, w_down
     )
@@ -385,7 +393,7 @@
         functools.partial(kernel, cols),
         out_shape=jax.ShapeDtypeStruct((rows, 128), jnp.float32),
         in_specs=[hbm] * 9,
-        out_specs=vmem,
+        out_specs=hbm,
         scratch_shapes=[
             (pltpu.SMEM if n in (1, 2) else pltpu.VMEM)(array.shape, array.dtype)
             for n, array in enumerate(operands)
@@ -401,7 +409,8 @@
             pltpu.VMEM((2, GROUPS, LR_TILES, 8, 128), jnp.bfloat16),
             pltpu.VMEM((2, GROUPS, TRI_TILES, 8, 128), jnp.bfloat16),
             pltpu.VMEM((2, GROUPS, TRI_TILES, 8, 128), jnp.bfloat16),
-            pltpu.SemaphoreType.DMA((9,)),
+            pltpu.VMEM((rows, 128), jnp.float32),
+            pltpu.SemaphoreType.DMA((12,)),
             pltpu.SemaphoreType.DMA((4, GROUPS)),
             pltpu.SemaphoreType.DMA((4, GROUPS)),
         ],

time: 43.2 us -> 42.4 us (0.981)
  Pallas kernels: 41.3 us -> 40.5 us
    pallas_call x1, Pallas kernels: 41.3 us -> 40.5 us  [split_channels(): pl.pallas_call(functools.partial(kernel, cols), out_shape=jax.ShapeDtypeS...]
where the time goes in v4:
time: 42.4 us; the launch traced here: 42.2 us
  Pallas kernels  40.5 us (96%)
  local copies, waits for them, and re-layouts  1.73 us (4%)
    pallas_call x1, Pallas kernels, split_channels(): pl.pallas_call(functools.partial(kernel, cols), out_shape=jax.ShapeDtypeS...  40.5 us
    reshape x1, local copies, waits for them, and re-layouts, split_channels(): return result.reshape(pair.shape[1], pair.shape[0], 128).swapaxes(0, 1)  1.73 us

profile of v4, /device:TPU:0, one launch (start us, length us, event | category | flops | bytes accessed | tf_op | source)
XLA Modules:
  0.0 42.2 jit_solution(3047426401271820171)
XLA Ops:
  0.0 40.5 %shard_map.91 = f32[576,128]{1,0:T(8,128)} custom-call(f32[576,128]{1,0:T(8,128)} %bitcast.6, s32[96]{0:T(128)} %chain_hbm.1, s32[12,12]{1,0:T(8,128)} %block_hbm.1, f32[5,128]{1,0:T(8,128)} %gain_hbm.1, f32[5,128]{1,0:T(8,128)} %bias_hbm.1, bf16[2,128,640]{2,1,0:T(8,128)(2,1)} %proj_hbm.1, bf16[2,128,128]{2,1,0:T(8,128)(2,1)} %out_hbm.1, ...), custom_call_target="tpu_custom_call" | custom-call | flops 900000000 | bytes 2000000 | tf_op jit(solution)/shard_map/pallas_call | solution.py:392
  40.5 1.7 %copy.12 = f32[24,24,128]{2,0,1:T(8,128)} copy(f32[24,24,128]{2,1,0:T(8,128)} %bitcast.5) | data formatting | bytes 589824 | tf_op jit(solution)/shard_map/reshape | solution.py:424
